TPU v7x, 32 devices: a whole 2x2x4 slice. The times are simulated.
32 devices in a mesh: grp: 2 (over x), dp: 2 (over core), tp: 8 (over z, y).
Axes of the slice: x: 2, y: 2, z: 4, core: 2. Of those that a mesh axis runs over, the one named last changes fastest.
Arguments:
- query_inputs: bfloat16 [4096, 8192], P(('grp', 'dp'), 'tp'), parts along dimension 0, may hold values from -250 to 250
- output_inputs: bfloat16 [4096, 8192], P(('grp', 'dp'), 'tp'), parts along dimension 0, may hold values from -250 to 250
- query_cotangent: bfloat16 [4096, 8192], P(('grp', 'dp'), 'tp'), parts along dimension 0, may hold values from -250 to 250
- output_cotangent: bfloat16 [4096, 8192], P(('grp', 'dp'), 'tp'), parts along dimension 0, may hold values from -250 to 250
- completion: int32 [4096], P(('grp', 'dp')), parts along dimension 0, may hold values from 0 to 15, never falling along the last dimension, each value on 1 to 256 neighbouring positions
- rewards: float32 [32], P('grp'), parts along dimension 0, may hold values from 0 to 1
- query_down: float32 [16384, 64], P(('grp', 'tp')), parts along dimension 0, may hold values from -0.0625 to 0.0625
- query_up: float32 [128, 8192], P('grp', 'tp'), parts along dimension 0, may hold values from -0.1875 to 0.1875
- output_down: float32 [16384, 64], P(('grp', 'tp')), parts along dimension 0, may hold values from -0.0625 to 0.0625
- output_up: float32 [128, 8192], P('grp', 'tp'), parts along dimension 0, may hold values from -0.1875 to 0.1875
- query_fixed_weight: bfloat16 [8192, 8192], P('dp', 'tp'), may hold values from -0.0625 to 0.0625
- output_fixed_weight: bfloat16 [8192, 8192], P('tp', 'dp'), may hold values from -0.09375 to 0.09375
- keyval_frozen: bfloat16 [8192, 2048], P('tp'), may hold values from -0.0625 to 0.0625
- decode_states: bfloat16 [4, 32, 8192], P(None, ('grp', 'dp'), 'tp'), parts along dimension 1, may hold values from -6 to 6
- key_cache: bfloat16 [32, 8, 64, 128], P(('grp', 'dp', 'tp')), parts along dimension 0, may hold values from -400 to 400
- value_cache: bfloat16 [32, 8, 64, 128], P(('grp', 'dp', 'tp')), parts along dimension 0, may hold values from -6 to 6
- cache_lengths: int32 [32], P(('grp', 'dp')), parts along dimension 0, may hold values from 2 to 64, as said below
Outputs:
- decoded: bfloat16 [4, 32, 8192], P(None, ('grp', 'dp'), 'tp'), parts along dimension 1
- new_query_down: float32 [16384, 64], P(('grp', 'tp')), parts along dimension 0
- new_query_up: float32 [128, 8192], P('grp', 'tp'), parts along dimension 0
- new_output_down: float32 [16384, 64], P(('grp', 'tp')), parts along dimension 0
- new_output_up: float32 [128, 8192], P('grp', 'tp'), parts along dimension 0
There are 2 independent parts, one for each index of `grp`. A program takes and returns all parts, laid end to end along the dimension named above; an argument that names none is the same for every part. Nothing has to cross between parts.
Inputs may be any that keep to these rules, and one draw needn't show every extreme that they name: Tokens of one completion are contiguous and completion numbers never fall along the tokens; a completion has 1 to 256 tokens. Row r uses the cached positions below cache_lengths[r]; some row uses all 64.
All inputs are finite; a program needn't handle non-finite values.
Results may differ from a plain program's by a relative error of at most 0.028.
Values may be sent and summed in bfloat16 or wider, within the bound.
A program may use at most 192 MiB of HBM per device.

v0:
```python
import math

import jax
import jax.numpy as jnp
from jax import lax
from jax.sharding import PartitionSpec as P

HEADS = 64
KVH = 8
HD = 128


adapter_scale_factor = 2.0
learn_rate = 8.0
clip_norm = 1.0


def attend(queries, cache_keys, cache_values, new_keys, new_values, valid_lengths, decode_step):
    score_scale = 1.0 / math.sqrt(queries.shape[-1])
    s_cache = (
        jnp.einsum("bgmd,bgcd->bgmc", queries, cache_keys, preferred_element_type=jnp.float32)
        * score_scale
    )
    s_new = (
        jnp.einsum("bgmd,bsgd->bgms", queries, new_keys, preferred_element_type=jnp.float32)
        * score_scale
    )
    cache_ok = (jnp.arange(cache_keys.shape[2], dtype=jnp.int32)[None, :] < valid_lengths[:, None])[
        :, None, None, :
    ]
    new_ok = (jnp.arange(new_keys.shape[1], dtype=jnp.int32) <= decode_step)[None, None, None, :]
    s_cache = jnp.where(cache_ok, s_cache, -jnp.inf)
    s_new = jnp.where(new_ok, s_new, -jnp.inf)
    highest = jnp.maximum(jnp.max(s_cache, axis=-1), jnp.max(s_new, axis=-1))[..., None]
    e_cache = jnp.exp(s_cache - highest)
    e_new = jnp.exp(s_new - highest)
    denominator = jnp.sum(e_cache, axis=-1, keepdims=True) + jnp.sum(e_new, axis=-1, keepdims=True)
    p_cache = (e_cache / denominator).astype(jnp.bfloat16)
    p_new = (e_new / denominator).astype(jnp.bfloat16)
    result = jnp.einsum(
        "bgmc,bgcd->bgmd", p_cache, cache_values, preferred_element_type=jnp.float32
    )
    result = result + jnp.einsum(
        "bgms,bsgd->bgmd", p_new, new_values, preferred_element_type=jnp.float32
    )
    return result.astype(jnp.bfloat16)


def weighted(token_weight, values_in):
    return (token_weight[:, None] * values_in).astype(jnp.bfloat16)


def across(left, right):
    return lax.dot_general(
        left, right, (((0,), (0,)), ((), ())), preferred_element_type=jnp.float32
    )


def against(left, right):
    return lax.dot_general(
        left, right, (((1,), (1,)), ((), ())), preferred_element_type=jnp.float32
    )


def squares(gradients):
    return sum((jnp.sum(gradient * gradient) for gradient in gradients))


def on_device(
    query_inputs,
    output_inputs,
    query_cotangent,
    output_cotangent,
    completion,
    rewards,
    query_down,
    query_up,
    output_down,
    output_up,
    query_fixed_weight,
    output_fixed_weight,
    keyval_frozen,
    decode_states,
    key_cache,
    value_cache,
    cache_lengths,
):
    advantage = rewards - jnp.mean(rewards)
    labels = jnp.arange(rewards.shape[0], dtype=jnp.int32)
    token_weight = jnp.sum(
        jnp.where(completion[:, None] == labels[None, :], advantage[None, :], 0.0), axis=1
    )
    down_q = query_down.astype(jnp.bfloat16)
    up_q = query_up.astype(jnp.bfloat16)
    down_o = output_down.astype(jnp.bfloat16)
    up_o = output_up.astype(jnp.bfloat16)
    partials = (
        jnp.dot(query_inputs, down_q, preferred_element_type=jnp.float32),
        against(query_cotangent, up_q),
        jnp.dot(output_inputs, down_o, preferred_element_type=jnp.float32),
        against(output_cotangent, up_o),
    )
    inner_query, back_query, inner_output, back_output = (
        lax.psum(partials[0].astype(jnp.bfloat16), "tp").astype(jnp.float32),
        lax.psum(partials[1].astype(jnp.bfloat16), "tp").astype(jnp.float32),
        lax.psum(partials[2].astype(jnp.bfloat16), "tp").astype(jnp.float32),
        lax.psum(partials[3].astype(jnp.bfloat16), "tp").astype(jnp.float32),
    )
    terms = (
        across(query_inputs, weighted(token_weight, back_query)),
        across(query_cotangent, weighted(token_weight, inner_query)),
        across(output_inputs, weighted(token_weight, back_output)),
        across(output_cotangent, weighted(token_weight, inner_output)),
    )
    current = (query_down, query_up.T, output_down, output_up.T)
    gradients = (
        lax.psum(terms[0].astype(jnp.bfloat16), "dp").astype(jnp.float32),
        lax.psum(terms[1].astype(jnp.bfloat16), "dp").astype(jnp.float32),
        lax.psum(terms[2].astype(jnp.bfloat16), "dp").astype(jnp.float32),
        lax.psum(terms[3].astype(jnp.bfloat16), "dp").astype(jnp.float32),
    )
    total_sq = lax.psum(squares(gradients), "tp")
    shrink = clip_norm / (jnp.sqrt(total_sq) + 1e-06)
    updated = tuple(
        (
            factor_state - learn_rate * shrink * gradient
            for factor_state, gradient in zip(current, gradients)
        )
    )
    new_query_down = updated[0]
    new_query_up = updated[1].T
    new_output_down = updated[2]
    new_output_up = updated[3].T
    rollout_down_q = new_query_down.astype(jnp.bfloat16)
    rollout_up_q = new_query_up.astype(jnp.bfloat16)
    rollout_down_o = new_output_down.astype(jnp.bfloat16)
    rollout_up_o = new_output_up.astype(jnp.bfloat16)
    full_down_q, full_up_o = (
        lax.all_gather(rollout_down_q, "tp", axis=0, tiled=True),
        lax.all_gather(rollout_up_o, "tp", axis=1, tiled=True),
    )
    steps_count, row_count, local_width = decode_states.shape
    query_width = query_fixed_weight.shape[1]
    tp_count = lax.axis_size("tp")
    tp_rank = lax.axis_index("tp")
    adapter_weight_delta = jnp.dot(full_down_q, rollout_up_q, preferred_element_type=jnp.float32)
    query_combined_weight = (
        lax.all_gather(query_fixed_weight, "dp", axis=0, tiled=True).astype(jnp.float32)
        + adapter_scale_factor * adapter_weight_delta
    ).astype(jnp.bfloat16)
    adapter_weight_delta = jnp.dot(rollout_down_o, full_up_o, preferred_element_type=jnp.float32)
    output_combined_weight = (
        lax.all_gather(output_fixed_weight, "dp", axis=1, tiled=True).astype(jnp.float32)
        + adapter_scale_factor * adapter_weight_delta
    ).astype(jnp.bfloat16)
    queries = jnp.einsum(
        "srd,dh->srh",
        lax.all_gather(decode_states, "tp", axis=2, tiled=True),
        query_combined_weight,
        preferred_element_type=jnp.float32,
    ).astype(jnp.bfloat16)
    fresh_part = jnp.einsum(
        "srd,dk->srk", decode_states, keyval_frozen, preferred_element_type=jnp.float32
    )
    part_heads = query_width // HD
    group_heads = HEADS // KVH
    new_entries = lax.psum(fresh_part.astype(jnp.bfloat16), "tp")
    kv_head = tp_rank * part_heads // group_heads
    own_keys = lax.dynamic_slice_in_dim(new_entries, kv_head * HD, HD, 2)
    own_values = lax.dynamic_slice_in_dim(new_entries, (KVH + kv_head) * HD, HD, 2)
    copies = tp_count // KVH
    spread_keys = jnp.repeat(key_cache, copies, axis=1)
    spread_values = jnp.repeat(value_cache, copies, axis=1)
    head_keys, head_values = (
        lax.all_to_all(spread_keys, "tp", split_axis=1, concat_axis=0, tiled=True),
        lax.all_to_all(spread_values, "tp", split_axis=1, concat_axis=0, tiled=True),
    )
    query_heads = queries.reshape(steps_count, row_count, 1, part_heads, HD)
    step_keys = jnp.transpose(own_keys, (1, 0, 2))[:, :, None, :]
    step_values = jnp.transpose(own_values, (1, 0, 2))[:, :, None, :]
    results = [
        attend(
            query_heads[decode_step],
            head_keys,
            head_values,
            step_keys,
            step_values,
            cache_lengths,
            decode_step,
        )
        for decode_step in range(steps_count)
    ]
    attended = jnp.stack(results).reshape(steps_count, row_count, query_width)
    flattened = attended.reshape(steps_count * row_count, query_width)
    local_columns = output_combined_weight.shape[1] // tp_count
    summed_out = lax.psum_scatter(
        lax.dot_general(
            output_combined_weight,
            flattened,
            (((0,), (1,)), ((), ())),
            preferred_element_type=jnp.float32,
        ).astype(jnp.bfloat16),
        "tp",
        scatter_dimension=0,
        tiled=True,
    ).astype(jnp.float32)
    decoded = summed_out.T.reshape(steps_count, row_count, local_columns).astype(jnp.bfloat16)
    return (decoded, new_query_down, new_query_up, new_output_down, new_output_up)


def solution(mesh):
    return jax.shard_map(
        on_device,
        mesh=mesh,
        in_specs=(
            P(("grp", "dp"), "tp"),
            P(("grp", "dp"), "tp"),
            P(("grp", "dp"), "tp"),
            P(("grp", "dp"), "tp"),
            P(("grp", "dp")),
            P("grp"),
            P(("grp", "tp"), None),
            P("grp", "tp"),
            P(("grp", "tp"), None),
            P("grp", "tp"),
            P("dp", "tp"),
            P("tp", "dp"),
            P("tp", None),
            P(None, ("grp", "dp"), "tp"),
            P(("grp", "dp", "tp"), None, None, None),
            P(("grp", "dp", "tp"), None, None, None),
            P(("grp", "dp")),
        ),
        out_specs=(
            P(None, ("grp", "dp"), "tp"),
            P(("grp", "tp"), None),
            P("grp", "tp"),
            P(("grp", "tp"), None),
            P("grp", "tp"),
        ),
        check_vma=False,
    )
```

profile of v0, /device:TPU:12, one launch (start us, length us, event | category | flops | bytes accessed | tf_op | source)
XLA Modules:
  0.0 375.6 jit_solution(8545084001275581679)
XLA Ops:
  7.2 3.2 convolution_convert_fusion.1
  10.4 2.5 convolution_convert_fusion.3
  13.0 1.4 convolution_convert_fusion.5
  14.4 1.4 convolution_convert_fusion.7
  15.8 1.5 fusion.12
  18.7 74.5 %all-reduce.5.cloned.1.call-done = (bf16[1024,64]{0,1:T(8,128)(2,1)}, bf16[1024,64]{0,1:T(8,128)(2,1)}, bf16[1024,64]{0,1:T(8,128)(2,1)}, bf16[1024,64]{0,1:T(8,128)(2,1)}, bf16[4,8,2048]{2,1,0:T(8,128)(2,1)}) async-done(((bf16[1024,64]{0,1:T(8,128)(2,1)}, bf16[1024,64]{0,1:T(8,128)(2,1)}, bf16[1024,64]{0,1:T(8,128)(2,1)}, bf16[1024,64]{0,1:T(8,128)(2,1)}, bf16[4,8,2048]{2,1,0:T(8,128)(2,1)}), ...) | async-done | bytes 655376 | tf_op jit(solution)/shard_map/psum | solution.py:106
  93.2 2.2 fusion.15
  95.4 1.1 fusion.16
  98.9 18.5 %all-reduce.7.cloned.1.call-done = (bf16[1024,64]{0,1:T(8,128)(2,1)}, bf16[1024,64]{0,1:T(8,128)(2,1)}, bf16[1024,64]{0,1:T(8,128)(2,1)}, bf16[1024,64]{0,1:T(8,128)(2,1)}) async-done(((bf16[1024,64]{0,1:T(8,128)(2,1)}, bf16[1024,64]{0,1:T(8,128)(2,1)}, bf16[1024,64]{0,1:T(8,128)(2,1)}, bf16[1024,64]{0,1:T(8,128)(2,1)}), (bf16[1024,64]{0,1:T(8,128)(2,1)}, bf16[1024,64]{0,1:T(8,128)(2,1)}, ...) | async-done | bytes 524304 | tf_op jit(solution)/shard_map/psum | solution.py:120
  117.4 1.6 fusion.41
  120.4 1.6 fusion.46
  123.3 15.5 %psum.78 = f32[]{:T(128)} all-reduce(f32[]{:T(128)S(6)} %add.100), channel_id=1, replica_groups=mesh['grp'=2,'dp'=2,'tp'=8] {'tp'}, use_global_device_ids=true, to_apply=%region_14.15 | all-reduce | flops 1 | bytes 8 | tf_op jit(solution)/shard_map/psum | solution.py:122
  139.6 1.7 fusion.119
  143.7 10.2 %all-to-all-start = ((bf16[1,8,64,128]{3,2,0,1:T(8,128)(2,1)}), bf16[1,8,64,128]{3,2,0,1:T(8,128)(2,1)S(1)}, u32[]{:S(2)}, u32[]{:S(2)}) async-start(bf16[1,8,64,128]{3,2,0,1:T(8,128)(2,1)} %bitcast.11), calls=%async_computation | async-start | bytes 262144 | tf_op jit(solution)/shard_map/all_to_all | solution.py:175
  154.0 29.4 %all_gather.19 = bf16[4,8,8192]{2,1,0:T(8,128)(2,1)S(1)} all-gather(bf16[4,8,1024]{2,1,0:T(8,128)(2,1)S(1)} %copy-done.15), channel_id=1, replica_groups=mesh['grp'=2,'dp'=2,'tp'=8] {'tp'}, dimensions={2}, use_global_device_ids=true | all-gather | bytes 589824 | tf_op jit(solution)/shard_map/all_gather | solution.py:158
  184.2 2.6 all-gather.11.cloned.1.call-done
  186.8 31.7 %all-gather.9.cloned.1.call-done = bf16[8192,1024]{1,0:T(8,128)(2,1)} async-done(((bf16[4096,1024]{1,0:T(8,128)(2,1)}), bf16[8192,1024]{1,0:T(8,128)(2,1)}) %all-gather.9.cloned.1.call-update) | async-done | bytes 16777232 | tf_op jit(solution)/shard_map/all_gather | solution.py:148
  218.5 11.2 %fusion.22 = bf16[4,8,1024]{2,1,0:T(8,128)(2,1)S(1)} fusion(bf16[4,8,8192]{2,1,0:T(8,128)(2,1)S(1)} %all_gather.19, bf16[8192,1024]{1,0:T(8,128)(2,1)} %all-gather.9.cloned.1.call-done, bf16[8192,64]{0,1:T(8,128)(2,1)} %all-gather.11.cloned.1.call-done, f32[64,1024]{1,0:T(8,128)S(1)} %fusion.45), kind=kOutput, calls=%fused_computation.25 | convolution fusion | flops 1644265472 | bytes 18677760 | tf_op jit(solution)/shard_map/srd,dh->srh/dot_general | solution.py:156
  229.9 6.1 %all-to-all-start.1 = ((bf16[1,8,64,128]{3,2,0,1:T(8,128)(2,1)}), bf16[1,8,64,128]{3,2,0,1:T(8,128)(2,1)S(1)}, u32[]{:S(2)}, u32[]{:S(2)}) async-start(bf16[1,8,64,128]{3,2,0,1:T(8,128)(2,1)} %bitcast.15), calls=%async_computation.1 | async-start | bytes 262144 | tf_op jit(solution)/shard_map/all_to_all | solution.py:176
  238.3 3.7 all-to-all-done.1
  243.6 17.4 %all-gather.7.cloned.1.call-done = bf16[64,8192]{1,0:T(8,128)(2,1)} async-done(((bf16[64,1024]{1,0:T(8,128)(2,1)}), bf16[64,8192]{1,0:T(8,128)(2,1)}) %all-gather.7.cloned.1.call-update) | async-done | bytes 1048592 | tf_op jit(solution)/shard_map/all_gather | solution.py:140
  261.0 32.4 %all-gather.5.cloned.1.call-done = bf16[1024,8192]{1,0:T(8,128)(2,1)} async-done(((bf16[1024,4096]{1,0:T(8,128)(2,1)}), bf16[1024,8192]{1,0:T(8,128)(2,1)}) %all-gather.5.cloned.1.call-update) | async-done | bytes 16777232 | tf_op jit(solution)/shard_map/all_gather | solution.py:153
  293.4 11.9 %fusion.9 = bf16[8192,32]{0,1:T(8,128)(2,1)} fusion(bf16[1024,8192]{1,0:T(8,128)(2,1)} %all-gather.5.cloned.1.call-done, bf16[64,8192]{1,0:T(8,128)(2,1)} %all-gather.7.cloned.1.call-done, f32[1024,64]{0,1:T(8,128)S(1)} %fusion.47, bf16[4,8,8,128]{3,2,1,0:T(8,128)(2,1)S(1)} %maximum_bitcast_fusion), kind=kOutput, calls=%fused_computation.8 | convolution fusion | flops 1644494848 | bytes 18677760 | tf_op jit(solution)/shard_map/dot_general | solution.py:197
  305.4 63.3 %reduce-scatter.2.cloned.1.call-done = bf16[1024,32]{0,1:T(8,128)(2,1)} async-done(((bf16[8192,32]{0,1:T(8,128)(2,1)}), bf16[1024,32]{0,1:T(8,128)(2,1)}) %reduce-scatter.2.cloned.1.call-update) | async-done | bytes 65552 | tf_op jit(solution)/shard_map/reduce_scatter | solution.py:196
  (111 shorter events, 10.5 us)
Async XLA Ops:
  7.2 5.8 %copy-start = (bf16[1024,1024]{1,0:T(8,128)(2,1)S(1)}, bf16[1024,1024]{1,0:T(8,128)(2,1)}, u32[]{:S(2)}) copy-start(bf16[1024,1024]{1,0:T(8,128)(2,1)} %param.17) | copy-start | bytes 6291460
  7.2 5.8 %copy-start.10 = (f32[1024,64]{0,1:T(8,128)S(1)}, f32[1024,64]{0,1:T(8,128)}, u32[]{:S(2)}) copy-start(f32[1024,64]{0,1:T(8,128)} %param.23) | copy-start | bytes 786436
  7.2 86.0 %all-reduce.5.cloned.1.call-start = ((), (), s32[]{:S(2)}) async-start(), calls=%async_computation.8 | async-start | bytes 1310720 | tf_op jit(solution)/shard_map/psum | solution.py:106
  7.2 3.2 copy-start.5
  10.4 4.0 %copy-start.2 = (bf16[1024,1024]{1,0:T(8,128)(2,1)S(1)}, bf16[1024,1024]{1,0:T(8,128)(2,1)}, u32[]{:S(2)}) copy-start(bf16[1024,1024]{1,0:T(8,128)(2,1)} %param.19) | copy-start | bytes 6291460
  10.4 4.0 %copy-start.8 = (f32[64,1024]{1,0:T(8,128)S(1)}, f32[64,1024]{1,0:T(8,128)}, u32[]{:S(2)}) copy-start(f32[64,1024]{1,0:T(8,128)} %param.24) | copy-start | bytes 786436
  13.0 2.9 copy-start.15
  17.3 100.1 %all-reduce.7.cloned.1.call-start = ((), (), s32[]{:S(2)}) async-start(), calls=%async_computation.9 | async-start | bytes 1048576 | tf_op jit(solution)/shard_map/psum | solution.py:120
  93.2 3.4 copy-start.4
  93.2 3.4 copy-start.19
  98.9 87.9 %all-gather.11.cloned.1.call-start = ((), (), s32[]{:S(2)}) async-start(), calls=%async_computation.6 | async-start | bytes 1179648 | tf_op jit(solution)/shard_map/all_gather | solution.py:139
  141.3 77.2 %all-gather.9.cloned.1.call-start = ((), (), s32[]{:S(2)}) async-start(), calls=%async_computation.5 | async-start | bytes 25165824 | tf_op jit(solution)/shard_map/all_gather | solution.py:148
  141.9 119.1 %all-gather.7.cloned.1.call-start = ((), (), s32[]{:S(2)}) async-start(), calls=%async_computation.4 | async-start | bytes 1179648 | tf_op jit(solution)/shard_map/all_gather | solution.py:140
  143.1 10.8 %copy-start.23 = (s32[8]{0:T(128)S(1)}, s32[8]{0:T(128)}, u32[]{:S(2)}) copy-start(s32[8]{0:T(128)} %param.33) | copy-start | bytes 100
  143.1 41.0 %copy-start.13 = (bf16[1024,64]{0,1:T(8,128)(2,1)S(1)}, bf16[1024,64]{0,1:T(8,128)(2,1)}, u32[]{:S(2)}) copy-start(bf16[1024,64]{0,1:T(8,128)(2,1)} %get-tuple-element.12) | copy-start | bytes 393220
  143.1 41.1 %copy-start.9 = (f32[1024,64]{0,1:T(8,128)S(1)}, f32[1024,64]{0,1:T(8,128)}, u32[]{:S(2)}) copy-start(f32[1024,64]{0,1:T(8,128)} %param.25) | copy-start | bytes 786436
  143.1 41.1 %copy-start.12 = (bf16[1024,64]{0,1:T(8,128)(2,1)S(1)}, bf16[1024,64]{0,1:T(8,128)(2,1)}, u32[]{:S(2)}) copy-start(bf16[1024,64]{0,1:T(8,128)(2,1)} %get-tuple-element.13) | copy-start | bytes 393220
  143.1 150.3 %all-gather.5.cloned.1.call-start = ((), (), s32[]{:S(2)}) async-start(), calls=%async_computation.3 | async-start | bytes 25165824 | tf_op jit(solution)/shard_map/all_gather | solution.py:153
  143.7 86.2 %all-to-all-start = ((bf16[1,8,64,128]{3,2,0,1:T(8,128)(2,1)}), bf16[1,8,64,128]{3,2,0,1:T(8,128)(2,1)S(1)}, u32[]{:S(2)}, u32[]{:S(2)}) async-start(bf16[1,8,64,128]{3,2,0,1:T(8,128)(2,1)} %bitcast.11), calls=%async_computation | async-start | bytes 262144 | tf_op jit(solution)/shard_map/all_to_all | solution.py:175
  184.2 45.6 %copy-start.16 = (f32[64,1024]{1,0:T(8,128)}, f32[64,1024]{1,0:T(8,128)S(1)}, u32[]{:S(2)}) copy-start(f32[64,1024]{1,0:T(8,128)S(1)} %fusion.45) | copy-start | bytes 786436
  184.2 109.2 %copy-start.17 = (f32[1024,64]{0,1:T(8,128)}, f32[1024,64]{0,1:T(8,128)S(1)}, u32[]{:S(2)}) copy-start(f32[1024,64]{0,1:T(8,128)S(1)} %fusion.47) | copy-start | bytes 786436
  229.9 12.0 %all-to-all-start.1 = ((bf16[1,8,64,128]{3,2,0,1:T(8,128)(2,1)}), bf16[1,8,64,128]{3,2,0,1:T(8,128)(2,1)S(1)}, u32[]{:S(2)}, u32[]{:S(2)}) async-start(bf16[1,8,64,128]{3,2,0,1:T(8,128)(2,1)} %bitcast.15), calls=%async_computation.1 | async-start | bytes 262144 | tf_op jit(solution)/shard_map/all_to_all | solution.py:176
  235.9 132.8 %reduce-scatter.2.cloned.1.call-start = ((), (), s32[]{:S(2)}) async-start(), calls=%async_computation.7 | async-start | bytes 589824 | tf_op jit(solution)/shard_map/reduce_scatter | solution.py:196
  293.4 75.3 %copy-start.1 = (bf16[1024,1024]{1,0:T(8,128)(2,1)S(1)}, bf16[1024,1024]{1,0:T(8,128)(2,1)}, u32[]{:S(2)}) copy-start(bf16[1024,1024]{1,0:T(8,128)(2,1)} %param.17) | copy-start | bytes 6291460
  (9 other events, 18.1 us)
Sparse Core Ops, SparseCore 0:
  17.4 75.7 all-reduce.4
  99.0 18.3 all-reduce.6
  141.4 45.3 all-gather.10
  188.2 30.3 all-gather.8
  220.6 40.4 all-gather.6
  262.4 30.9 all-gather.4
  305.5 63.1 reduce-scatter.1
where the time goes:
time: 378 us; the launch traced here: 376 us
  waiting for transfers between devices  245 us (65%)
  blocking collectives  44.9 us (12%)
  matrix products  41.9 us (11%)
  between operations  18.4 us (5%)
  starting transfers between devices  16.5 us (4%)
  other arithmetic  7.43 us (2%)
    psum x1, waiting for transfers between devices, on_device(): lax.psum(partials[2].astype(jnp.bfloat16), 'tp').astype(jnp.float32)  74.5 us
    reduce_scatter x1, waiting for transfers between devices, on_device(): lax.psum_scatter(lax.dot_general(output_combined_weight, flattened, (((0,...  63.3 us
    all_gather x1, waiting for transfers between devices, on_device(): lax.all_gather(output_fixed_weight, 'dp', axis=1, tiled=True)  32.4 us
    all_gather x1, waiting for transfers between devices, on_device(): lax.all_gather(query_fixed_weight, 'dp', axis=0, tiled=True)  31.7 us
    all_gather x1, blocking collectives, on_device(): lax.all_gather(decode_states, 'tp', axis=2, tiled=True)  29.4 us
    psum x1, waiting for transfers between devices, on_device(): lax.psum(terms[3].astype(jnp.bfloat16), 'dp').astype(jnp.float32)  18.5 us
    all_gather x1, waiting for transfers between devices, on_device(): lax.all_gather(rollout_up_o, 'tp', axis=1, tiled=True)  17.4 us
    psum x1, blocking collectives, on_device(): total_sq = lax.psum(squares(gradients), 'tp')  15.5 us
  transfers between devices with their start and end apart: 9, of which 8 were waited for; matrix products, arithmetic and copies ran while one was open for 5% of the time, Pallas kernels for 0%

commit v1 on v0

--- a/solution.py
+++ b/solution.py
@@ -3,6 +3,8 @@
 import jax
 import jax.numpy as jnp
 from jax import lax
+from jax.experimental import pallas as pl
+from jax.experimental.pallas import tpu as pltpu
 from jax.sharding import PartitionSpec as P
 
 HEADS = 64
@@ -208,9 +210,498 @@
     return (decoded, new_query_down, new_query_up, new_output_down, new_output_up)
 
 
+MESH = pl.DeviceIdType.MESH
+RANK = 64
+LANES = 128
+COLS = 256
+
+
+def dot_nn(left, right):
+    return jnp.dot(left, right, preferred_element_type=jnp.float32)
+
+
+def landed(ref, sem):
+    pltpu.make_async_copy(ref, ref, sem).wait()
+
+
+def fused_kernel(
+    n,
+    xq,
+    cq,
+    xo,
+    co,
+    wq_hbm,
+    wo_hbm,
+    kv_hbm,
+    states,
+    kc,
+    vc,
+    token_weight,
+    bias,
+    qd,
+    qu,
+    od,
+    ou,
+    dec,
+    new_qd,
+    new_qu,
+    new_od,
+    new_ou,
+    act,
+    wq,
+    wo,
+    kv,
+    factors,
+    part,
+    rs,
+    own_w,
+    wfull,
+    gs,
+    gr,
+    gsum,
+    kall,
+    vall,
+    ne_src,
+    ne_recv,
+    stf,
+    small,
+    small_recv,
+    qp,
+    qr,
+    attall,
+    al,
+    al_recv,
+    osrc,
+    orecv,
+    load_sem,
+    kv_send,
+    kv_recv,
+    rs_send,
+    rs_recv,
+    ag_send,
+    ag_recv,
+    ne_sems,
+    st_sems,
+    g_send,
+    g_recv,
+    small_sems,
+    q_sems,
+    att_sems,
+    al_sems,
+    o_sems,
+):
+    d = lax.axis_index("dp")
+    t = lax.axis_index("tp")
+    other = 1 - d
+    half = n // 2
+    width = act.shape[2]
+    rows = states.shape[0]
+    cache = kc.shape[1]
+    peers = [lax.rem(t + k, n) for k in range(n)]
+
+    def load(source, target, index):
+        pltpu.make_async_copy(source, target, load_sem.at[index]).start()
+
+    def send(source, target, send_sem, recv_sem, device):
+        pltpu.make_async_remote_copy(
+            src_ref=source,
+            dst_ref=target,
+            send_sem=send_sem,
+            recv_sem=recv_sem,
+            device_id=device,
+            device_id_type=MESH,
+        ).start()
+
+    for index, source in enumerate((xq, cq, xo, co)):
+        load(source, act.at[index], index)
+    load(kv_hbm, kv, 4)
+
+    barrier = pltpu.get_barrier_semaphore()
+    for k in range(n):
+        if k > 0:
+            pl.semaphore_signal(barrier, inc=1, device_id={"tp": peers[k]}, device_id_type=MESH)
+        pl.semaphore_signal(
+            barrier, inc=1, device_id={"dp": other, "tp": peers[k]}, device_id_type=MESH
+        )
+
+    factors[0] = qd[...].T.astype(jnp.bfloat16)
+    factors[1] = qu[...].astype(jnp.bfloat16)
+    factors[2] = od[...].T.astype(jnp.bfloat16)
+    factors[3] = ou[...].astype(jnp.bfloat16)
+
+    pl.semaphore_wait(barrier, 2 * n - 1)
+
+    own_cache = pl.ds(pl.multiple_of(t * cache, cache), cache)
+    for k in range(1, n):
+        send(kc.at[peers[k]], kall.at[own_cache], kv_send.at[0], kv_recv.at[0], {"tp": peers[k]})
+        send(vc.at[peers[k]], vall.at[own_cache], kv_send.at[1], kv_recv.at[1], {"tp": peers[k]})
+    kall[own_cache, :] = kc[t]
+    vall[own_cache, :] = vc[t]
+
+    def project(m, carry):
+        landed(act.at[m], load_sem.at[m])
+        for c in range(width // COLS):
+            block = against(factors[m], act[m, c * COLS : (c + 1) * COLS, :]).astype(jnp.bfloat16)
+            for i in range(COLS // LANES):
+                part[m, c * (COLS // LANES) + i] = block[:, i * LANES : (i + 1) * LANES]
+        for k in range(1, n):
+            send(
+                part.at[m, peers[k]],
+                rs.at[m, k - 1],
+                rs_send.at[m],
+                rs_recv.at[m],
+                {"tp": peers[k]},
+            )
+        return carry
+
+    lax.fori_loop(0, 4, project, 0)
+
+    load(wq_hbm, wq, 5)
+    load(wo_hbm, wo, 6)
+
+    landed(kv, load_sem.at[4])
+    for c in range(2 * n * HD // COLS):
+        block = dot_nn(states[...], kv[:, c * COLS : (c + 1) * COLS]).astype(jnp.bfloat16)
+        for i in range(COLS // HD):
+            head = c * (COLS // HD) + i
+            ne_src[head % n, head // n] = block[:, i * HD : (i + 1) * HD]
+
+    own_tokens = pl.ds(pl.multiple_of(t * LANES, LANES), LANES)
+
+    def reduce_weight(m, carry):
+        landed(rs.at[m], rs_recv.at[m])
+        total = part[m, t].astype(jnp.float32)
+        for k in range(n - 1):
+            total = total + rs[m, k].astype(jnp.float32)
+        block = (total * token_weight[t]).astype(jnp.bfloat16)
+        own_w[m] = block
+        wfull[m, :, own_tokens] = block
+        for k in range(1, n):
+            send(
+                own_w.at[m],
+                wfull.at[m, :, own_tokens],
+                ag_send.at[m],
+                ag_recv.at[m],
+                {"tp": peers[k]},
+            )
+        return carry
+
+    lax.fori_loop(0, 4, reduce_weight, 0)
+
+    for k in range(1, n):
+        send(ne_src.at[peers[k]], ne_recv.at[k - 1], ne_sems.at[0], ne_sems.at[1], {"tp": peers[k]})
+
+    home = lax.div(t, half)
+    stays = home == d
+    st_place = stf.at[lax.rem(t, half), pl.ds(pl.multiple_of(d * rows, rows), rows)]
+    for k in range(1, n):
+        send(states, st_place, st_sems.at[0], st_sems.at[1], {"dp": home, "tp": peers[k]})
+
+    @pl.when(stays)
+    def _():
+        pltpu.make_async_copy(states, st_place, st_sems.at[1]).start()
+
+    @pl.when(jnp.logical_not(stays))
+    def _():
+        send(states, st_place, st_sems.at[0], st_sems.at[1], {"dp": other})
+
+    others = pl.ds(0, (n - 1) * LANES)
+
+    def gradient(i, carry):
+        m = i + 1 - 2 * lax.rem(i, 2)
+        landed(wfull.at[i, :, others], ag_recv.at[i])
+        for c in range(width // COLS):
+            at = slice(c * COLS, (c + 1) * COLS)
+            gs[m, :, at] = dot_nn(wfull[i], act[m, :, at]).astype(jnp.bfloat16)
+        send(gs.at[m], gr.at[m], g_send.at[m], g_recv.at[m], {"dp": other})
+        return carry
+
+    lax.fori_loop(0, 4, gradient, 0)
+
+    squared = jnp.zeros((8, LANES), jnp.float32)
+    for m in (1, 0, 3, 2):
+        landed(gr.at[m], g_recv.at[m])
+        total = gs[m].astype(jnp.float32) + gr[m].astype(jnp.float32)
+        gsum[m] = total
+        square = total * total
+        for a in range(RANK // 8):
+            for b in range(width // LANES):
+                squared = squared + square[a * 8 : (a + 1) * 8, b * LANES : (b + 1) * LANES]
+    small[:rows, :RANK] = against(states[...], gsum[0].astype(jnp.bfloat16))
+    small[:rows, RANK:] = against(states[...], factors[0])
+    small[rows:, :] = squared
+    for k in range(1, n):
+        send(small, small_recv.at[k - 1], small_sems.at[0], small_sems.at[1], {"tp": peers[k]})
+
+    landed(stf, st_sems.at[1])
+    landed(wq, load_sem.at[5])
+
+    def queries(c, carry):
+        at = pl.ds(pl.multiple_of(c * COLS, COLS), COLS)
+        total = dot_nn(stf[0], wq[0:width, at])
+        for j in range(1, half):
+            total = total + dot_nn(stf[j], wq[j * width : (j + 1) * width, at])
+        qp[0, :, at] = total[:rows]
+        qp[1, :, at] = total[rows:]
+        return carry
+
+    lax.fori_loop(0, width // COLS, queries, 0)
+    send(qp.at[other], qr, q_sems.at[0], q_sems.at[1], {"dp": other})
+
+    landed(ne_recv, ne_sems.at[1])
+    fresh = ne_src[t].astype(jnp.float32)
+    for k in range(n - 1):
+        fresh = fresh + ne_recv[k].astype(jnp.float32)
+    fresh = fresh.astype(jnp.bfloat16)
+
+    landed(small_recv, small_sems.at[1])
+    total = small[...]
+    for k in range(n - 1):
+        total = total + small_recv[k]
+    norm = jnp.sqrt(jnp.sum(total[rows:, :], axis=(0, 1), keepdims=True))
+    step = learn_rate * (clip_norm / (norm + 1e-06))
+    new_up_q = qu[...] - step * gsum[1]
+    new_qu[...] = new_up_q
+    inner = (total[:rows, RANK:] - step * total[:rows, :RANK]).astype(jnp.bfloat16)
+    lora = dot_nn(inner, new_up_q.astype(jnp.bfloat16))
+
+    landed(qr, q_sems.at[1])
+    query = (qp[d] + qr[...] + adapter_scale_factor * lora).astype(jnp.bfloat16)
+    heads = width // HD
+    stacked = jnp.concatenate([query[:, h * HD : (h + 1) * HD] for h in range(heads)], axis=0)
+
+    landed(kall.at[pl.ds(0, (n - 1) * cache)], kv_recv.at[0])
+    landed(vall.at[pl.ds(0, (n - 1) * cache)], kv_recv.at[1])
+    count = rows * heads
+    scale = 1.0 / math.sqrt(HD)
+    low = jnp.float32(-1e30)
+    s_old = against(stacked, kall[...]) * scale + bias[...]
+    s_new = against(stacked, fresh[0]) * scale
+    row_old = lax.broadcasted_iota(jnp.int32, s_old.shape, 0)
+    col_old = lax.broadcasted_iota(jnp.int32, s_old.shape, 1)
+    s_old = jnp.where(jnp.bitwise_and(row_old, n - 1) == lax.div(col_old, cache), s_old, low)
+    row_new = lax.broadcasted_iota(jnp.int32, s_new.shape, 0)
+    col_new = lax.broadcasted_iota(jnp.int32, s_new.shape, 1)
+    same = jnp.bitwise_and(row_new, n - 1) == jnp.bitwise_and(col_new, n - 1)
+    known = col_new <= jnp.bitwise_and(row_new, rows - 1)
+    s_new = jnp.where(jnp.logical_and(same, known), s_new, low)
+    highest = jnp.maximum(
+        jnp.max(s_old, axis=1, keepdims=True), jnp.max(s_new, axis=1, keepdims=True)
+    )
+    e_old = jnp.exp(s_old - highest)
+    e_new = jnp.exp(s_new - highest)
+    denominator = jnp.sum(e_old, axis=1, keepdims=True) + jnp.sum(e_new, axis=1, keepdims=True)
+    result = dot_nn((e_old / denominator).astype(jnp.bfloat16), vall[...])
+    result = result + dot_nn((e_new / denominator).astype(jnp.bfloat16), fresh[1])
+    result = result.astype(jnp.bfloat16)
+    attended = jnp.concatenate(
+        [result[h * rows : (h + 1) * rows, :] for h in range(heads)], axis=1
+    )
+    attall[d] = attended
+    send(attall.at[d], attall.at[d], att_sems.at[0], att_sems.at[1], {"dp": other})
+
+    down_step = step * gsum[2]
+    new_down_o = od[...].T - down_step
+    al[:, :RANK] = against(attended, new_down_o.astype(jnp.bfloat16))
+    al[:, RANK:] = jnp.zeros((rows, LANES - RANK), jnp.float32)
+    for k in range(1, n):
+        send(al, al_recv.at[k - 1], al_sems.at[0], al_sems.at[1], {"tp": peers[k]})
+
+    landed(wo, load_sem.at[6])
+    landed(attall.at[other], att_sems.at[1])
+    both = attall[...].reshape(2 * rows, width)
+
+    def outputs(j, carry):
+        for c in range(width // COLS):
+            at = pl.ds(pl.multiple_of(j * width + c * COLS, COLS), COLS)
+            block = dot_nn(both, wo[:, at]).astype(jnp.bfloat16)
+            osrc[j, 0, :, c * COLS : (c + 1) * COLS] = block[:rows]
+            osrc[j, 1, :, c * COLS : (c + 1) * COLS] = block[rows:]
+        owner = half * d + j
+        send(
+            osrc.at[j, other],
+            orecv.at[t],
+            o_sems.at[0],
+            o_sems.at[1],
+            {"dp": other, "tp": owner},
+        )
+        mine = owner == t
+
+        @pl.when(mine)
+        def _():
+            pltpu.make_async_copy(osrc.at[j, d], orecv.at[t], o_sems.at[1]).start()
+
+        @pl.when(jnp.logical_not(mine))
+        def _():
+            send(osrc.at[j, d], orecv.at[t], o_sems.at[0], o_sems.at[1], {"tp": owner})
+
+        return carry
+
+    lax.fori_loop(0, half, outputs, 0)
+
+    new_up_o = ou[...] - step * gsum[3]
+    new_ou[...] = new_up_o
+    new_od[...] = new_down_o.T
+    new_qd[...] = qd[...] - (step * gsum[0]).T
+
+    landed(al_recv, al_sems.at[1])
+    inner = al[...]
+    for k in range(n - 1):
+        inner = inner + al_recv[k]
+    lora = dot_nn(inner[:, :RANK].astype(jnp.bfloat16), new_up_o.astype(jnp.bfloat16))
+
+    landed(orecv, o_sems.at[1])
+    total = adapter_scale_factor * lora
+    for k in range(n):
+        total = total + orecv[k].astype(jnp.float32)
+    dec[...] = total.astype(jnp.bfloat16)
+
+    landed(kall.at[pl.ds(0, (n - 1) * cache)], kv_send.at[0])
+    landed(vall.at[pl.ds(0, (n - 1) * cache)], kv_send.at[1])
+    for m in range(4):
+        landed(rs.at[m], rs_send.at[m])
+        landed(wfull.at[m, :, others], ag_send.at[m])
+        landed(gs.at[m], g_send.at[m])
+    landed(ne_recv, ne_sems.at[0])
+    landed(small_recv, small_sems.at[0])
+    landed(qr, q_sems.at[0])
+    landed(attall.at[d], att_sems.at[0])
+    landed(al_recv, al_sems.at[0])
+    landed(orecv.at[pl.ds(0, n - 1)], o_sems.at[0])
+    for k in range(n - 1):
+        landed(states, st_sems.at[0])
+
+    @pl.when(jnp.logical_not(stays))
+    def _():
+        landed(states, st_sems.at[0])
+        landed(orecv.at[0], o_sems.at[0])
+
+
+def fused(
+    query_inputs,
+    output_inputs,
+    query_cotangent,
+    output_cotangent,
+    completion,
+    rewards,
+    query_down,
+    query_up,
+    output_down,
+    output_up,
+    query_fixed_weight,
+    output_fixed_weight,
+    keyval_frozen,
+    decode_states,
+    key_cache,
+    value_cache,
+    cache_lengths,
+):
+    n = lax.axis_size("tp")
+    tokens, width = query_inputs.shape
+    steps_count, row_count, _ = decode_states.shape
+    rows = steps_count * row_count
+    cache = key_cache.shape[2]
+    advantage = rewards - jnp.mean(rewards)
+    labels = jnp.arange(rewards.shape[0], dtype=jnp.int32)
+    token_weight = jnp.sum(
+        jnp.where(completion[:, None] == labels[None, :], advantage[None, :], 0.0), axis=1
+    ).reshape(n, 1, tokens // n)
+    valid = jnp.arange(cache, dtype=jnp.int32)[None, :] < cache_lengths[:, None]
+    bias = jnp.where(valid, 0.0, -1e30).astype(jnp.float32).reshape(1, row_count * cache)
+    vmem = pl.BlockSpec(memory_space=pltpu.VMEM)
+    hbm = pl.BlockSpec(memory_space=pl.ANY)
+    bf16, f32 = jnp.bfloat16, jnp.float32
+    dma = pltpu.SemaphoreType.DMA
+    outs = pl.pallas_call(
+        lambda *refs: fused_kernel(n, *refs),
+        out_shape=(
+            jax.ShapeDtypeStruct((rows, width), bf16),
+            jax.ShapeDtypeStruct(query_down.shape, f32),
+            jax.ShapeDtypeStruct(query_up.shape, f32),
+            jax.ShapeDtypeStruct(output_down.shape, f32),
+            jax.ShapeDtypeStruct(output_up.shape, f32),
+        ),
+        in_specs=[hbm] * 7 + [vmem] * 9,
+        out_specs=(vmem,) * 5,
+        scratch_shapes=[
+            pltpu.VMEM((4, tokens, width), bf16),
+            pltpu.VMEM(query_fixed_weight.shape, bf16),
+            pltpu.VMEM(output_fixed_weight.shape, bf16),
+            pltpu.VMEM(keyval_frozen.shape, bf16),
+            pltpu.VMEM((4, RANK, width), bf16),
+            pltpu.VMEM((4, n, RANK, LANES), bf16),
+            pltpu.VMEM((4, n - 1, RANK, LANES), bf16),
+            pltpu.VMEM((4, RANK, LANES), bf16),
+            pltpu.VMEM((4, RANK, tokens), bf16),
+            pltpu.VMEM((4, RANK, width), bf16),
+            pltpu.VMEM((4, RANK, width), bf16),
+            pltpu.VMEM((4, RANK, width), f32),
+            pltpu.VMEM((n * cache, HD), bf16),
+            pltpu.VMEM((n * cache, HD), bf16),
+            pltpu.VMEM((n, 2, rows, HD), bf16),
+            pltpu.VMEM((n - 1, 2, rows, HD), bf16),
+            pltpu.VMEM((n // 2, 2 * rows, width), bf16),
+            pltpu.VMEM((rows + 8, LANES), f32),
+            pltpu.VMEM((n - 1, rows + 8, LANES), f32),
+            pltpu.VMEM((2, rows, width), f32),
+            pltpu.VMEM((rows, width), f32),
+            pltpu.VMEM((2, rows, width), bf16),
+            pltpu.VMEM((rows, LANES), f32),
+            pltpu.VMEM((n - 1, rows, LANES), f32),
+            pltpu.VMEM((n // 2, 2, rows, width), bf16),
+            pltpu.VMEM((n, rows, width), bf16),
+            dma((7,)),
+            dma((2,)),
+            dma((2,)),
+            dma((4,)),
+            dma((4,)),
+            dma((4,)),
+            dma((4,)),
+            dma((2,)),
+            dma((2,)),
+            dma((4,)),
+            dma((4,)),
+            dma((2,)),
+            dma((2,)),
+            dma((2,)),
+            dma((2,)),
+            dma((2,)),
+        ],
+        compiler_params=pltpu.CompilerParams(
+            collective_id=0, has_side_effects=True, vmem_limit_bytes=56 << 20
+        ),
+        cost_estimate=pl.CostEstimate(
+            flops=4 * 10**9, bytes_accessed=36 * 10**6, transcendentals=1 << 17
+        ),
+    )(
+        query_inputs,
+        query_cotangent,
+        output_inputs,
+        output_cotangent,
+        query_fixed_weight,
+        output_fixed_weight,
+        keyval_frozen,
+        decode_states.reshape(rows, width),
+        key_cache[0],
+        value_cache[0],
+        token_weight,
+        bias,
+        query_down,
+        query_up,
+        output_down,
+        output_up,
+    )
+    decoded = outs[0].reshape(steps_count, row_count, width)
+    return (decoded, *outs[1:])
+
+
+def fits(mesh):
+    return mesh.shape["dp"] == 2 and mesh.shape["tp"] == KVH
+
+
 def solution(mesh):
     return jax.shard_map(
-        on_device,
+        fused if fits(mesh) else on_device,
         mesh=mesh,
         in_specs=(
             P(("grp", "dp"), "tp"),

time: 378 us -> 89.4 us (0.24)
  waiting for transfers between devices: 245 us -> 0 us
  Pallas kernels: 0 us -> 71.3 us
  blocking collectives: 44.9 us -> 0 us
  matrix products: 41.9 us -> 0 us
  between operations: 18.4 us -> 1.3 us
  starting transfers between devices: 16.5 us -> 0 us
  local copies, waits for them, and re-layouts: 1.18 us -> 12.3 us
    psum x2 -> x0, waiting for transfers between devices: 93 us -> none  [the longest x1 74.5 us: on_device(): lax.psum(partials[2].astype(jnp.bfloat16), 'tp').astype(jnp.float32)]
    all_gather x4 -> x0, waiting for transfers between devices: 84.1 us -> none  [the longest x1 32.4 us: on_device(): lax.all_gather(output_fixed_weight, 'dp', axis=1, tiled=True)]
    pallas_call x0 -> x1, Pallas kernels: none -> 71.3 us  [fused(): pl.pallas_call(lambda *refs: fused_kernel(n, *refs), out_shape=(jax.Shape...]
    reduce_scatter x1 -> x0, waiting for transfers between devices: 63.3 us -> none  [on_device(): lax.psum_scatter(lax.dot_general(output_combined_weight, flattened, (((0,...]
    dot_general x27 -> x0, matrix products: 41.9 us -> none  [the longest x1 11.9 us: on_device(): lax.dot_general(output_combined_weight, flattened, (((0,), (1,)), ((), ()...]
    all_gather x1 -> x0, blocking collectives: 29.4 us -> none  [on_device(): lax.all_gather(decode_states, 'tp', axis=2, tiled=True)]
    all_to_all x2 -> x0, starting transfers between devices: 16.2 us -> none  [the longest x1 10.2 us: on_device(): lax.all_to_all(spread_keys, 'tp', split_axis=1, concat_axis=0, tiled=True)]
    psum x1 -> x0, blocking collectives: 15.5 us -> none  [on_device(): total_sq = lax.psum(squares(gradients), 'tp')]
  transfers between devices with their start and end apart: 9 -> 0, of which waited for: 8 -> 0; matrix products, arithmetic and copies ran while one was open for 5% -> 0% of each run, Pallas kernels for 0% -> 0%
where the time goes in v1:
time: 89.4 us; the launch traced here: 88.9 us
  Pallas kernels  71.3 us (80%)
  local copies, waits for them, and re-layouts  12.3 us (14%)
  other arithmetic  4.01 us (4%)
  between operations  1.3 us (1%)
    pallas_call x1, Pallas kernels, fused(): pl.pallas_call(lambda *refs: fused_kernel(n, *refs), out_shape=(jax.Shape...  71.3 us
    unnamed x9, local copies, waits for them, and re-layouts  11.7 us

profile of v1, /device:TPU:12, one launch (start us, length us, event | category | flops | bytes accessed | tf_op | source)
XLA Modules:
  0.0 88.9 jit_solution(13774753590985642182)
XLA Ops:
  0.6 1.3 %reduce_sum.18 = f32[]{:T(128)} reduce(f32[16]{0:T(128)} %param.22, f32[]{:T(128)} %constant.1.clone.1), dimensions={0}, to_apply=%region_0.0 | reduce | flops 15 | bytes 72 | tf_op jit(solution)/shard_map/reduce_sum | solution.py:604
  2.5 0.7 broadcast_subtract_fusion
  3.2 1.4 %select_reduce_fusion = f32[1024]{0:T(1024)} fusion(f32[16]{0:T(128)S(1)} %broadcast_subtract_fusion, s32[1024]{0:T(1024)} %param.21), kind=kLoop, calls=%fused_computation | loop fusion | flops 48128 | bytes 8256 | tf_op jit(solution)/shard_map/reduce_sum | solution.py:606
  4.6 0.7 fusion
  5.3 0.7 select_n.20.refs_11_
  5.9 1.9 %copy.26.refs_12_ = f32[1024,64]{1,0:T(8,128)} copy(f32[1024,64]{0,1:T(8,128)} %param.23) | data formatting | bytes 524288 | tf_op args[6]
  7.9 2.0 %copy.27.refs_14_ = f32[1024,64]{1,0:T(8,128)} copy(f32[1024,64]{0,1:T(8,128)} %param.25) | data formatting | bytes 524288 | tf_op args[8]
  9.9 71.3 %shard_map.200 = (bf16[32,1024]{1,0:T(8,128)(2,1)}, f32[1024,64]{1,0:T(8,128)}, f32[64,1024]{1,0:T(8,128)}, f32[1024,64]{1,0:T(8,128)}, f32[64,1024]{1,0:T(8,128)}) custom-call(bf16[1024,1024]{1,0:T(8,128)(2,1)} %refs_0_.1, bf16[1024,1024]{1,0:T(8,128)(2,1)} %refs_1_.1, bf16[1024,1024]{1,0:T(8,128)(2,1)} %refs_2_.1, bf16[1024,1024]{1,0:T(8,128)(2,1)} %refs_3_.1, ...), custom_call_target="tpu_custom_call" | custom-call | flops 4000000000 | bytes 36000000 | tf_op jit(solution)/shard_map/pallas_call | solution.py:615
  81.2 0.0 copy-start
  81.2 2.0 %copy.28 = f32[1024,64]{0,1:T(8,128)} copy(f32[1024,64]{1,0:T(8,128)} %get-tuple-element.21) | data formatting | bytes 524288
  83.2 1.9 %copy.29 = f32[1024,64]{0,1:T(8,128)} copy(f32[1024,64]{1,0:T(8,128)} %get-tuple-element.23) | data formatting | bytes 524288
  85.1 1.5 %copy.33 = bf16[4,8,1024]{2,1,0:T(8,128)(2,1)} copy(bf16[4,8,1024]{2,1,0:T(8,128)(2,1)} %bitcast.8) | data formatting | bytes 131072
  86.6 1.7 %copy.34 = f32[64,1024]{1,0:T(8,128)} copy(f32[64,1024]{1,0:T(8,128)} %get-tuple-element.32) | data formatting | bytes 524288
  88.2 0.0 copy-done
  88.2 0.7 copy.35
Async XLA Ops:
  81.2 7.1 %copy-start = (f32[64,1024]{1,0:T(8,128)S(1)}, f32[64,1024]{1,0:T(8,128)}, u32[]{:S(2)}) copy-start(f32[64,1024]{1,0:T(8,128)} %get-tuple-element.34) | copy-start | bytes 786436

commit v2 on v1

--- a/solution.py
+++ b/solution.py
@@ -233,20 +233,22 @@
     wq_hbm,
     wo_hbm,
     kv_hbm,
-    states,
+    states_hbm,
     kc,
     vc,
-    token_weight,
-    bias,
-    qd,
-    qu,
-    od,
-    ou,
+    completion,
+    rewards,
+    lengths,
+    qd_hbm,
+    qu_hbm,
+    od_hbm,
+    ou_hbm,
+    dec_out,
+    new_out,
+    states,
+    held,
+    updated,
     dec,
-    new_qd,
-    new_qu,
-    new_od,
-    new_ou,
     act,
     wq,
     wo,
@@ -289,6 +291,7 @@
     att_sems,
     al_sems,
     o_sems,
+    out_sems,
 ):
     d = lax.axis_index("dp")
     t = lax.axis_index("tp")
@@ -312,6 +315,9 @@
             device_id_type=MESH,
         ).start()
 
+    load(states_hbm, states, 7)
+    for index, source in enumerate((qd_hbm, qu_hbm, od_hbm, ou_hbm)):
+        load(source, held.at[index], 8 + index)
     for index, source in enumerate((xq, cq, xo, co)):
         load(source, act.at[index], index)
     load(kv_hbm, kv, 4)
@@ -324,10 +330,18 @@
             barrier, inc=1, device_id={"dp": other, "tp": peers[k]}, device_id_type=MESH
         )
 
-    factors[0] = qd[...].T.astype(jnp.bfloat16)
-    factors[1] = qu[...].astype(jnp.bfloat16)
-    factors[2] = od[...].T.astype(jnp.bfloat16)
-    factors[3] = ou[...].astype(jnp.bfloat16)
+    for m in range(4):
+        landed(held.at[m], load_sem.at[8 + m])
+        factors[m] = held[m].astype(jnp.bfloat16)
+    count = rewards.shape[0]
+    mean = rewards[0]
+    for c in range(1, count):
+        mean = mean + rewards[c]
+    mean = mean / count
+    own_completion = completion[t]
+    token_weight = jnp.zeros(own_completion.shape, jnp.float32)
+    for c in range(count):
+        token_weight = jnp.where(own_completion == c, rewards[c] - mean, token_weight)
 
     pl.semaphore_wait(barrier, 2 * n - 1)
 
@@ -335,8 +349,8 @@
     for k in range(1, n):
         send(kc.at[peers[k]], kall.at[own_cache], kv_send.at[0], kv_recv.at[0], {"tp": peers[k]})
         send(vc.at[peers[k]], vall.at[own_cache], kv_send.at[1], kv_recv.at[1], {"tp": peers[k]})
-    kall[own_cache, :] = kc[t]
-    vall[own_cache, :] = vc[t]
+    load(kc.at[t], kall.at[own_cache], 12)
+    load(vc.at[t], vall.at[own_cache], 13)
 
     def project(m, carry):
         landed(act.at[m], load_sem.at[m])
@@ -359,6 +373,7 @@
     load(wq_hbm, wq, 5)
     load(wo_hbm, wo, 6)
 
+    landed(states, load_sem.at[7])
     landed(kv, load_sem.at[4])
     for c in range(2 * n * HD // COLS):
         block = dot_nn(states[...], kv[:, c * COLS : (c + 1) * COLS]).astype(jnp.bfloat16)
@@ -373,7 +388,7 @@
         total = part[m, t].astype(jnp.float32)
         for k in range(n - 1):
             total = total + rs[m, k].astype(jnp.float32)
-        block = (total * token_weight[t]).astype(jnp.bfloat16)
+        block = (total * token_weight).astype(jnp.bfloat16)
         own_w[m] = block
         wfull[m, :, own_tokens] = block
         for k in range(1, n):
@@ -460,26 +475,34 @@
         total = total + small_recv[k]
     norm = jnp.sqrt(jnp.sum(total[rows:, :], axis=(0, 1), keepdims=True))
     step = learn_rate * (clip_norm / (norm + 1e-06))
-    new_up_q = qu[...] - step * gsum[1]
-    new_qu[...] = new_up_q
+    for m in range(4):
+        updated[m] = held[m] - step * gsum[m]
+        pltpu.make_async_copy(updated.at[m], new_out.at[m], out_sems.at[m]).start()
     inner = (total[:rows, RANK:] - step * total[:rows, :RANK]).astype(jnp.bfloat16)
-    lora = dot_nn(inner, new_up_q.astype(jnp.bfloat16))
+    lora = dot_nn(inner, updated[1].astype(jnp.bfloat16))
 
     landed(qr, q_sems.at[1])
     query = (qp[d] + qr[...] + adapter_scale_factor * lora).astype(jnp.bfloat16)
     heads = width // HD
     stacked = jnp.concatenate([query[:, h * HD : (h + 1) * HD] for h in range(heads)], axis=0)
 
+    landed(kall.at[own_cache], load_sem.at[12])
+    landed(vall.at[own_cache], load_sem.at[13])
     landed(kall.at[pl.ds(0, (n - 1) * cache)], kv_recv.at[0])
     landed(vall.at[pl.ds(0, (n - 1) * cache)], kv_recv.at[1])
-    count = rows * heads
     scale = 1.0 / math.sqrt(HD)
     low = jnp.float32(-1e30)
-    s_old = against(stacked, kall[...]) * scale + bias[...]
+    s_old = against(stacked, kall[...]) * scale
     s_new = against(stacked, fresh[0]) * scale
     row_old = lax.broadcasted_iota(jnp.int32, s_old.shape, 0)
-    col_old = lax.broadcasted_iota(jnp.int32, s_old.shape, 1)
-    s_old = jnp.where(jnp.bitwise_and(row_old, n - 1) == lax.div(col_old, cache), s_old, low)
+    column = lax.broadcasted_iota(jnp.int32, (1, n * cache), 1)
+    column_row = lax.div(column, cache)
+    column_length = jnp.zeros_like(column)
+    for r in range(n):
+        column_length = jnp.where(column_row == r, lengths[r], column_length)
+    usable = column - column_row * cache < column_length
+    target = jnp.where(usable, column_row, -1)
+    s_old = jnp.where(jnp.bitwise_and(row_old, n - 1) == target, s_old, low)
     row_new = lax.broadcasted_iota(jnp.int32, s_new.shape, 0)
     col_new = lax.broadcasted_iota(jnp.int32, s_new.shape, 1)
     same = jnp.bitwise_and(row_new, n - 1) == jnp.bitwise_and(col_new, n - 1)
@@ -500,9 +523,7 @@
     attall[d] = attended
     send(attall.at[d], attall.at[d], att_sems.at[0], att_sems.at[1], {"dp": other})
 
-    down_step = step * gsum[2]
-    new_down_o = od[...].T - down_step
-    al[:, :RANK] = against(attended, new_down_o.astype(jnp.bfloat16))
+    al[:, :RANK] = against(attended, updated[2].astype(jnp.bfloat16))
     al[:, RANK:] = jnp.zeros((rows, LANES - RANK), jnp.float32)
     for k in range(1, n):
         send(al, al_recv.at[k - 1], al_sems.at[0], al_sems.at[1], {"tp": peers[k]})
@@ -539,22 +560,18 @@
 
     lax.fori_loop(0, half, outputs, 0)
 
-    new_up_o = ou[...] - step * gsum[3]
-    new_ou[...] = new_up_o
-    new_od[...] = new_down_o.T
-    new_qd[...] = qd[...] - (step * gsum[0]).T
-
     landed(al_recv, al_sems.at[1])
     inner = al[...]
     for k in range(n - 1):
         inner = inner + al_recv[k]
-    lora = dot_nn(inner[:, :RANK].astype(jnp.bfloat16), new_up_o.astype(jnp.bfloat16))
+    lora = dot_nn(inner[:, :RANK].astype(jnp.bfloat16), updated[3].astype(jnp.bfloat16))
 
     landed(orecv, o_sems.at[1])
     total = adapter_scale_factor * lora
     for k in range(n):
         total = total + orecv[k].astype(jnp.float32)
     dec[...] = total.astype(jnp.bfloat16)
+    pltpu.make_async_copy(dec, dec_out, out_sems.at[4]).start()
 
     landed(kall.at[pl.ds(0, (n - 1) * cache)], kv_send.at[0])
     landed(vall.at[pl.ds(0, (n - 1) * cache)], kv_send.at[1])
@@ -562,6 +579,8 @@
         landed(rs.at[m], rs_send.at[m])
         landed(wfull.at[m, :, others], ag_send.at[m])
         landed(gs.at[m], g_send.at[m])
+        landed(updated.at[m], out_sems.at[m])
+    landed(dec, out_sems.at[4])
     landed(ne_recv, ne_sems.at[0])
     landed(small_recv, small_sems.at[0])
     landed(qr, q_sems.at[0])
@@ -575,6 +594,16 @@
     def _():
         landed(states, st_sems.at[0])
         landed(orecv.at[0], o_sems.at[0])
+
+
+def hand_over(dec, factors, dec_out, qd, qu, od, ou, sems):
+    copies = [pltpu.make_async_copy(dec, dec_out, sems.at[4])]
+    for m, target in enumerate((qd, qu, od, ou)):
+        copies.append(pltpu.make_async_copy(factors.at[m], target, sems.at[m]))
+    for copy in copies:
+        copy.start()
+    for copy in copies:
+        copy.wait()
 
 
 def fused(
@@ -601,14 +630,8 @@
     steps_count, row_count, _ = decode_states.shape
     rows = steps_count * row_count
     cache = key_cache.shape[2]
-    advantage = rewards - jnp.mean(rewards)
-    labels = jnp.arange(rewards.shape[0], dtype=jnp.int32)
-    token_weight = jnp.sum(
-        jnp.where(completion[:, None] == labels[None, :], advantage[None, :], 0.0), axis=1
-    ).reshape(n, 1, tokens // n)
-    valid = jnp.arange(cache, dtype=jnp.int32)[None, :] < cache_lengths[:, None]
-    bias = jnp.where(valid, 0.0, -1e30).astype(jnp.float32).reshape(1, row_count * cache)
     vmem = pl.BlockSpec(memory_space=pltpu.VMEM)
+    smem = pl.BlockSpec(memory_space=pltpu.SMEM)
     hbm = pl.BlockSpec(memory_space=pl.ANY)
     bf16, f32 = jnp.bfloat16, jnp.float32
     dma = pltpu.SemaphoreType.DMA
@@ -616,14 +639,15 @@
         lambda *refs: fused_kernel(n, *refs),
         out_shape=(
             jax.ShapeDtypeStruct((rows, width), bf16),
-            jax.ShapeDtypeStruct(query_down.shape, f32),
-            jax.ShapeDtypeStruct(query_up.shape, f32),
-            jax.ShapeDtypeStruct(output_down.shape, f32),
-            jax.ShapeDtypeStruct(output_up.shape, f32),
+            jax.ShapeDtypeStruct((4, RANK, width), f32),
         ),
-        in_specs=[hbm] * 7 + [vmem] * 9,
-        out_specs=(vmem,) * 5,
+        in_specs=[hbm] * 10 + [vmem, smem, smem] + [hbm] * 4,
+        out_specs=(hbm, hbm),
         scratch_shapes=[
+            pltpu.VMEM((rows, width), bf16),
+            pltpu.VMEM((4, RANK, width), f32),
+            pltpu.VMEM((4, RANK, width), f32),
+            pltpu.VMEM((rows, width), bf16),
             pltpu.VMEM((4, tokens, width), bf16),
             pltpu.VMEM(query_fixed_weight.shape, bf16),
             pltpu.VMEM(output_fixed_weight.shape, bf16),
@@ -650,7 +674,7 @@
             pltpu.VMEM((n - 1, rows, LANES), f32),
             pltpu.VMEM((n // 2, 2, rows, width), bf16),
             pltpu.VMEM((n, rows, width), bf16),
-            dma((7,)),
+            dma((14,)),
             dma((2,)),
             dma((2,)),
             dma((4,)),
@@ -666,6 +690,7 @@
             dma((2,)),
             dma((2,)),
             dma((2,)),
+            dma((5,)),
         ],
         compiler_params=pltpu.CompilerParams(
             collective_id=0, has_side_effects=True, vmem_limit_bytes=56 << 20
@@ -684,15 +709,26 @@
         decode_states.reshape(rows, width),
         key_cache[0],
         value_cache[0],
-        token_weight,
-        bias,
-        query_down,
+        completion.reshape(n, 1, tokens // n),
+        rewards,
+        cache_lengths,
+        query_down.T,
         query_up,
-        output_down,
+        output_down.T,
         output_up,
     )
-    decoded = outs[0].reshape(steps_count, row_count, width)
-    return (decoded, *outs[1:])
+    final = pl.pallas_call(
+        hand_over,
+        out_shape=(
+            jax.ShapeDtypeStruct((rows, width), bf16),
+            *[jax.ShapeDtypeStruct((RANK, width), f32)] * 4,
+        ),
+        in_specs=[hbm, hbm],
+        out_specs=(hbm,) * 5,
+        scratch_shapes=[dma((5,))],
+    )(*outs)
+    decoded = final[0].reshape(steps_count, row_count, width)
+    return (decoded, final[1].T, final[2], final[3].T, final[4])
 
 
 def fits(mesh):

time: 89.4 us -> 106 us (1.19)
  Pallas kernels: 71.3 us -> 105 us
  local copies, waits for them, and re-layouts: 12.3 us -> 0 us
  other arithmetic: 4.01 us -> 0 us
    pallas_call x0 -> x1, Pallas kernels: none -> 34.9 us  [fused(): pl.pallas_call(hand_over, out_shape=(jax.ShapeDtypeStruct((rows, width),...]
    unnamed x9 -> x0, local copies, waits for them, and re-layouts: 11.7 us -> none
    reduce_sum x2 -> x0, other arithmetic: 2.62 us -> none  [the longest x1 1.36 us: fused(): jnp.sum(jnp.where(completion[:, None] == labels[None, :], advantage[None,...]
where the time goes in v2:
time: 106 us
  Pallas kernels  105 us (99%)
    pallas_call x1, Pallas kernels, fused(): pl.pallas_call(lambda *refs: fused_kernel(n, *refs), out_shape=(jax.Shape...  70.5 us
    pallas_call x1, Pallas kernels, fused(): pl.pallas_call(hand_over, out_shape=(jax.ShapeDtypeStruct((rows, width),...  34.9 us

profile of v2, /device:TPU:12, one launch (start us, length us, event | category | flops | bytes accessed | tf_op | source)
XLA Modules:
  0.0 106.1 jit_solution(14479589953984685814)
XLA Ops:
  0.6 70.5 %shard_map.200 = (bf16[32,1024]{1,0:T(8,128)(2,1)}, f32[4,64,1024]{2,1,0:T(8,128)}) custom-call(bf16[1024,1024]{1,0:T(8,128)(2,1)} %refs_0_.1, bf16[1024,1024]{1,0:T(8,128)(2,1)} %refs_1_.1, bf16[1024,1024]{1,0:T(8,128)(2,1)} %refs_2_.1, bf16[1024,1024]{1,0:T(8,128)(2,1)} %refs_3_.1, bf16[4096,1024]{1,0:T(8,128)(2,1)} %refs_4_.1, ...), custom_call_target="tpu_custom_call" | custom-call | flops 4000000000 | bytes 36000000 | tf_op jit(solution)/shard_map/pallas_call | solution.py:638
  71.2 34.9 %shard_map.201 = (bf16[32,1024]{1,0:T(8,128)(2,1)}, f32[64,1024]{1,0:T(8,128)}, f32[64,1024]{1,0:T(8,128)}, f32[64,1024]{1,0:T(8,128)}, f32[64,1024]{1,0:T(8,128)}) custom-call(bf16[32,1024]{1,0:T(8,128)(2,1)} %get-tuple-element.12.dec, f32[4,64,1024]{2,1,0:T(8,128)} %get-tuple-element.13.factors), custom_call_target="tpu_custom_call" | custom-call | tf_op jit(solution)/shard_map/pallas_call | solution.py:720

commit v3 on v2

--- a/solution.py
+++ b/solution.py
@@ -253,8 +253,10 @@
     wq,
     wo,
     kv,
-    factors,
+    columns,
     part,
+    pair_part,
+    line_part,
     rs,
     own_w,
     wfull,
@@ -273,15 +275,20 @@
     attall,
     al,
     al_recv,
-    osrc,
+    opair,
+    opair_recv,
+    osum,
     orecv,
     load_sem,
     kv_send,
     kv_recv,
+    pair_send,
+    pair_recv,
     rs_send,
     rs_recv,
     ag_send,
-    ag_recv,
+    ag_line,
+    ag_pair,
     ne_sems,
     st_sems,
     g_send,
@@ -290,6 +297,8 @@
     q_sems,
     att_sems,
     al_sems,
+    opair_send,
+    opair_got,
     o_sems,
     out_sems,
 ):
@@ -301,6 +310,11 @@
     rows = states.shape[0]
     cache = kc.shape[1]
     peers = [lax.rem(t + k, n) for k in range(n)]
+    y = lax.rem(t, 2)
+    z = lax.div(t, 2)
+    pair = t + 1 - 2 * y
+    line = [lax.rem(t + 2 * k, n) for k in range(half)]
+    line_z = [lax.rem(z + k, half) for k in range(half)]
 
     def load(source, target, index):
         pltpu.make_async_copy(source, target, load_sem.at[index]).start()
@@ -332,7 +346,7 @@
 
     for m in range(4):
         landed(held.at[m], load_sem.at[8 + m])
-        factors[m] = held[m].astype(jnp.bfloat16)
+        columns[m] = held[m].T.astype(jnp.bfloat16)
     count = rewards.shape[0]
     mean = rewards[0]
     for c in range(1, count):
@@ -345,33 +359,58 @@
 
     pl.semaphore_wait(barrier, 2 * n - 1)
 
-    own_cache = pl.ds(pl.multiple_of(t * cache, cache), cache)
-    for k in range(1, n):
-        send(kc.at[peers[k]], kall.at[own_cache], kv_send.at[0], kv_recv.at[0], {"tp": peers[k]})
-        send(vc.at[peers[k]], vall.at[own_cache], kv_send.at[1], kv_recv.at[1], {"tp": peers[k]})
-    load(kc.at[t], kall.at[own_cache], 12)
-    load(vc.at[t], vall.at[own_cache], 13)
+    home = lax.div(t, half)
+    stays = home == d
+    st_place = stf.at[lax.rem(t, half), pl.ds(pl.multiple_of(d * rows, rows), rows)]
+    for k in range(1, half):
+        send(states_hbm, st_place, st_sems.at[0], st_sems.at[1], {"dp": home, "tp": line[k]})
+
+    @pl.when(stays)
+    def _():
+        pltpu.make_async_copy(states_hbm, st_place, st_sems.at[1]).start()
+
+    @pl.when(jnp.logical_not(stays))
+    def _():
+        send(states_hbm, st_place, st_sems.at[0], st_sems.at[1], {"dp": other})
 
     def project(m, carry):
         landed(act.at[m], load_sem.at[m])
         for c in range(width // COLS):
-            block = against(factors[m], act[m, c * COLS : (c + 1) * COLS, :]).astype(jnp.bfloat16)
+            block = dot_nn(act[m, c * COLS : (c + 1) * COLS, :], columns[m])
+            block = block.T.astype(jnp.bfloat16)
             for i in range(COLS // LANES):
-                part[m, c * (COLS // LANES) + i] = block[:, i * LANES : (i + 1) * LANES]
-        for k in range(1, n):
+                part[m, i, c] = block[:, i * LANES : (i + 1) * LANES]
+        send(part.at[m, 1 - y], pair_part.at[m], pair_send.at[m], pair_recv.at[m], {"tp": pair})
+        return carry
+
+    def pair_sum(m):
+        landed(pair_part.at[m], pair_recv.at[m])
+        for i in range(half):
+            total = part[m, y, i].astype(jnp.float32) + pair_part[m, i].astype(jnp.float32)
+            line_part[m, i] = total.astype(jnp.bfloat16)
+        for k in range(1, half):
             send(
-                part.at[m, peers[k]],
+                line_part.at[m, line_z[k]],
                 rs.at[m, k - 1],
                 rs_send.at[m],
                 rs_recv.at[m],
-                {"tp": peers[k]},
+                {"tp": line[k]},
             )
+
+    def project_and_sum(m, carry):
+        project(m, carry)
+        pair_sum(m - 1)
         return carry
 
-    lax.fori_loop(0, 4, project, 0)
-
+    project(0, 0)
     load(wq_hbm, wq, 5)
     load(wo_hbm, wo, 6)
+    lax.fori_loop(1, 4, project_and_sum, 0)
+    pair_sum(3)
+    landed(stf.at[pl.ds(0, half // 2)], st_sems.at[1])
+    for i in range(half // 2):
+        place = stf.at[2 * i + y]
+        send(place, place, st_sems.at[2], st_sems.at[3], {"tp": pair})
 
     landed(states, load_sem.at[7])
     landed(kv, load_sem.at[4])
@@ -381,50 +420,52 @@
             head = c * (COLS // HD) + i
             ne_src[head % n, head // n] = block[:, i * HD : (i + 1) * HD]
 
-    own_tokens = pl.ds(pl.multiple_of(t * LANES, LANES), LANES)
-
-    def reduce_weight(m, carry):
+    def tokens_of(owner):
+        return pl.ds(pl.multiple_of(owner * LANES, LANES), LANES)
+
+    def reduce_weight(m):
         landed(rs.at[m], rs_recv.at[m])
-        total = part[m, t].astype(jnp.float32)
-        for k in range(n - 1):
+        total = line_part[m, z].astype(jnp.float32)
+        for k in range(half - 1):
             total = total + rs[m, k].astype(jnp.float32)
         block = (total * token_weight).astype(jnp.bfloat16)
         own_w[m] = block
-        wfull[m, :, own_tokens] = block
-        for k in range(1, n):
-            send(
-                own_w.at[m],
-                wfull.at[m, :, own_tokens],
-                ag_send.at[m],
-                ag_recv.at[m],
-                {"tp": peers[k]},
-            )
+        place = wfull.at[m, :, tokens_of(t)]
+        wfull[m, :, tokens_of(t)] = block
+        for k in range(1, half):
+            send(own_w.at[m], place, ag_send.at[m], ag_line.at[m], {"tp": line[k]})
+        send(own_w.at[m], place, ag_send.at[m], ag_pair.at[m], {"tp": pair})
+
+    def forward(m):
+        landed(wfull.at[m, :, pl.ds(0, (half - 1) * LANES)], ag_line.at[m])
+        for k in range(1, half):
+            place = wfull.at[m, :, tokens_of(line[k])]
+            send(place, place, ag_send.at[m], ag_pair.at[m], {"tp": pair})
+
+    def weight_and_forward(m, carry):
+        reduce_weight(m)
+        forward(m - 1)
         return carry
 
-    lax.fori_loop(0, 4, reduce_weight, 0)
+    reduce_weight(0)
+    lax.fori_loop(1, 4, weight_and_forward, 0)
+    forward(3)
 
     for k in range(1, n):
         send(ne_src.at[peers[k]], ne_recv.at[k - 1], ne_sems.at[0], ne_sems.at[1], {"tp": peers[k]})
 
-    home = lax.div(t, half)
-    stays = home == d
-    st_place = stf.at[lax.rem(t, half), pl.ds(pl.multiple_of(d * rows, rows), rows)]
+    own_cache = pl.ds(pl.multiple_of(t * cache, cache), cache)
     for k in range(1, n):
-        send(states, st_place, st_sems.at[0], st_sems.at[1], {"dp": home, "tp": peers[k]})
-
-    @pl.when(stays)
-    def _():
-        pltpu.make_async_copy(states, st_place, st_sems.at[1]).start()
-
-    @pl.when(jnp.logical_not(stays))
-    def _():
-        send(states, st_place, st_sems.at[0], st_sems.at[1], {"dp": other})
+        send(kc.at[peers[k]], kall.at[own_cache], kv_send.at[0], kv_recv.at[0], {"tp": peers[k]})
+        send(vc.at[peers[k]], vall.at[own_cache], kv_send.at[1], kv_recv.at[1], {"tp": peers[k]})
+    load(kc.at[t], kall.at[own_cache], 12)
+    load(vc.at[t], vall.at[own_cache], 13)
 
     others = pl.ds(0, (n - 1) * LANES)
 
     def gradient(i, carry):
         m = i + 1 - 2 * lax.rem(i, 2)
-        landed(wfull.at[i, :, others], ag_recv.at[i])
+        landed(wfull.at[i, :, pl.ds(0, half * LANES)], ag_pair.at[i])
         for c in range(width // COLS):
             at = slice(c * COLS, (c + 1) * COLS)
             gs[m, :, at] = dot_nn(wfull[i], act[m, :, at]).astype(jnp.bfloat16)
@@ -443,12 +484,12 @@
             for b in range(width // LANES):
                 squared = squared + square[a * 8 : (a + 1) * 8, b * LANES : (b + 1) * LANES]
     small[:rows, :RANK] = against(states[...], gsum[0].astype(jnp.bfloat16))
-    small[:rows, RANK:] = against(states[...], factors[0])
+    small[:rows, RANK:] = dot_nn(states[...], columns[0])
     small[rows:, :] = squared
     for k in range(1, n):
         send(small, small_recv.at[k - 1], small_sems.at[0], small_sems.at[1], {"tp": peers[k]})
 
-    landed(stf, st_sems.at[1])
+    landed(stf.at[pl.ds(0, half // 2)], st_sems.at[3])
     landed(wq, load_sem.at[5])
 
     def queries(c, carry):
@@ -514,8 +555,9 @@
     e_old = jnp.exp(s_old - highest)
     e_new = jnp.exp(s_new - highest)
     denominator = jnp.sum(e_old, axis=1, keepdims=True) + jnp.sum(e_new, axis=1, keepdims=True)
-    result = dot_nn((e_old / denominator).astype(jnp.bfloat16), vall[...])
-    result = result + dot_nn((e_new / denominator).astype(jnp.bfloat16), fresh[1])
+    inverse = 1.0 / denominator
+    result = dot_nn((e_old * inverse).astype(jnp.bfloat16), vall[...])
+    result = result + dot_nn((e_new * inverse).astype(jnp.bfloat16), fresh[1])
     result = result.astype(jnp.bfloat16)
     attended = jnp.concatenate(
         [result[h * rows : (h + 1) * rows, :] for h in range(heads)], axis=1
@@ -532,16 +574,31 @@
     landed(attall.at[other], att_sems.at[1])
     both = attall[...].reshape(2 * rows, width)
 
-    def outputs(j, carry):
+    def product(j, c):
+        at = pl.ds(pl.multiple_of(j * width + c * COLS, COLS), COLS)
+        return dot_nn(both, wo[:, at])
+
+    def for_pair(i, carry):
         for c in range(width // COLS):
-            at = pl.ds(pl.multiple_of(j * width + c * COLS, COLS), COLS)
-            block = dot_nn(both, wo[:, at]).astype(jnp.bfloat16)
-            osrc[j, 0, :, c * COLS : (c + 1) * COLS] = block[:rows]
-            osrc[j, 1, :, c * COLS : (c + 1) * COLS] = block[rows:]
-        owner = half * d + j
+            at = slice(c * COLS, (c + 1) * COLS)
+            opair[i, :, at] = product(2 * i + 1 - y, c).astype(jnp.bfloat16)
+        send(opair.at[i], opair_recv.at[i], opair_send.at[i], opair_got.at[i], {"tp": pair})
+        return carry
+
+    lax.fori_loop(0, half // 2, for_pair, 0)
+
+    def for_line(i, carry):
+        landed(opair_recv.at[i], opair_got.at[i])
+        for c in range(width // COLS):
+            at = slice(c * COLS, (c + 1) * COLS)
+            block = product(2 * i + y, c).astype(jnp.bfloat16).astype(jnp.float32)
+            block = (block + opair_recv[i, :, at].astype(jnp.float32)).astype(jnp.bfloat16)
+            osum[i, 0, :, at] = block[:rows]
+            osum[i, 1, :, at] = block[rows:]
+        owner = half * d + 2 * i + y
         send(
-            osrc.at[j, other],
-            orecv.at[t],
+            osum.at[i, other],
+            orecv.at[z],
             o_sems.at[0],
             o_sems.at[1],
             {"dp": other, "tp": owner},
@@ -550,15 +607,15 @@
 
         @pl.when(mine)
         def _():
-            pltpu.make_async_copy(osrc.at[j, d], orecv.at[t], o_sems.at[1]).start()
+            pltpu.make_async_copy(osum.at[i, d], orecv.at[z], o_sems.at[1]).start()
 
         @pl.when(jnp.logical_not(mine))
         def _():
-            send(osrc.at[j, d], orecv.at[t], o_sems.at[0], o_sems.at[1], {"tp": owner})
+            send(osum.at[i, d], orecv.at[z], o_sems.at[0], o_sems.at[1], {"tp": owner})
 
         return carry
 
-    lax.fori_loop(0, half, outputs, 0)
+    lax.fori_loop(0, half // 2, for_line, 0)
 
     landed(al_recv, al_sems.at[1])
     inner = al[...]
@@ -568,7 +625,7 @@
 
     landed(orecv, o_sems.at[1])
     total = adapter_scale_factor * lora
-    for k in range(n):
+    for k in range(half):
         total = total + orecv[k].astype(jnp.float32)
     dec[...] = total.astype(jnp.bfloat16)
     pltpu.make_async_copy(dec, dec_out, out_sems.at[4]).start()
@@ -576,6 +633,7 @@
     landed(kall.at[pl.ds(0, (n - 1) * cache)], kv_send.at[0])
     landed(vall.at[pl.ds(0, (n - 1) * cache)], kv_send.at[1])
     for m in range(4):
+        landed(pair_part.at[m], pair_send.at[m])
         landed(rs.at[m], rs_send.at[m])
         landed(wfull.at[m, :, others], ag_send.at[m])
         landed(gs.at[m], g_send.at[m])
@@ -586,8 +644,11 @@
     landed(qr, q_sems.at[0])
     landed(attall.at[d], att_sems.at[0])
     landed(al_recv, al_sems.at[0])
-    landed(orecv.at[pl.ds(0, n - 1)], o_sems.at[0])
-    for k in range(n - 1):
+    for i in range(half // 2):
+        landed(opair.at[i], opair_send.at[i])
+    landed(orecv.at[pl.ds(0, half - 1)], o_sems.at[0])
+    landed(stf.at[pl.ds(0, half // 2)], st_sems.at[2])
+    for k in range(half - 1):
         landed(states, st_sems.at[0])
 
     @pl.when(jnp.logical_not(stays))
@@ -596,14 +657,10 @@
         landed(orecv.at[0], o_sems.at[0])
 
 
-def hand_over(dec, factors, dec_out, qd, qu, od, ou, sems):
-    copies = [pltpu.make_async_copy(dec, dec_out, sems.at[4])]
+def hand_over(dec, factors, dec_out, qd, qu, od, ou):
+    dec_out[...] = dec[...]
     for m, target in enumerate((qd, qu, od, ou)):
-        copies.append(pltpu.make_async_copy(factors.at[m], target, sems.at[m]))
-    for copy in copies:
-        copy.start()
-    for copy in copies:
-        copy.wait()
+        target[...] = factors[m]
 
 
 def fused(
@@ -652,9 +709,11 @@
             pltpu.VMEM(query_fixed_weight.shape, bf16),
             pltpu.VMEM(output_fixed_weight.shape, bf16),
             pltpu.VMEM(keyval_frozen.shape, bf16),
-            pltpu.VMEM((4, RANK, width), bf16),
-            pltpu.VMEM((4, n, RANK, LANES), bf16),
-            pltpu.VMEM((4, n - 1, RANK, LANES), bf16),
+            pltpu.VMEM((4, width, RANK), bf16),
+            pltpu.VMEM((4, 2, n // 2, RANK, LANES), bf16),
+            pltpu.VMEM((4, n // 2, RANK, LANES), bf16),
+            pltpu.VMEM((4, n // 2, RANK, LANES), bf16),
+            pltpu.VMEM((4, n // 2 - 1, RANK, LANES), bf16),
             pltpu.VMEM((4, RANK, LANES), bf16),
             pltpu.VMEM((4, RANK, tokens), bf16),
             pltpu.VMEM((4, RANK, width), bf16),
@@ -672,8 +731,10 @@
             pltpu.VMEM((2, rows, width), bf16),
             pltpu.VMEM((rows, LANES), f32),
             pltpu.VMEM((n - 1, rows, LANES), f32),
-            pltpu.VMEM((n // 2, 2, rows, width), bf16),
-            pltpu.VMEM((n, rows, width), bf16),
+            pltpu.VMEM((n // 4, 2 * rows, width), bf16),
+            pltpu.VMEM((n // 4, 2 * rows, width), bf16),
+            pltpu.VMEM((n // 4, 2, rows, width), bf16),
+            pltpu.VMEM((n // 2, rows, width), bf16),
             dma((14,)),
             dma((2,)),
             dma((2,)),
@@ -681,10 +742,15 @@
             dma((4,)),
             dma((4,)),
             dma((4,)),
-            dma((2,)),
-            dma((2,)),
-            dma((4,)),
-            dma((4,)),
+            dma((4,)),
+            dma((4,)),
+            dma((4,)),
+            dma((2,)),
+            dma((4,)),
+            dma((4,)),
+            dma((4,)),
+            dma((2,)),
+            dma((2,)),
             dma((2,)),
             dma((2,)),
             dma((2,)),
@@ -723,9 +789,8 @@
             jax.ShapeDtypeStruct((rows, width), bf16),
             *[jax.ShapeDtypeStruct((RANK, width), f32)] * 4,
         ),
-        in_specs=[hbm, hbm],
-        out_specs=(hbm,) * 5,
-        scratch_shapes=[dma((5,))],
+        in_specs=[vmem, vmem],
+        out_specs=(vmem,) * 5,
     )(*outs)
     decoded = final[0].reshape(steps_count, row_count, width)
     return (decoded, final[1].T, final[2], final[3].T, final[4])

time: 106 us -> 59.1 us (0.56)
  the two profiles are of different devices: /device:TPU:12 before, /device:TPU:0 now
where the time goes in v3:
time: 59.1 us; the launch traced here: 59 us
  Pallas kernels  58.3 us (99%)
  between operations  0.65 us (1%)
    pallas_call x1, Pallas kernels, fused(): pl.pallas_call(lambda *refs: fused_kernel(n, *refs), out_shape=(jax.Shape...  56 us
    pallas_call x1, Pallas kernels, fused(): pl.pallas_call(hand_over, out_shape=(jax.ShapeDtypeStruct((rows, width),...  2.27 us

profile of v3, /device:TPU:0, one launch (start us, length us, event | category | flops | bytes accessed | tf_op | source)
XLA Modules:
  0.0 59.0 jit_solution(3523285412857508287)
XLA Ops:
  0.6 56.0 %shard_map.200 = (bf16[32,1024]{1,0:T(8,128)(2,1)}, f32[4,64,1024]{2,1,0:T(8,128)}) custom-call(bf16[1024,1024]{1,0:T(8,128)(2,1)} %refs_0_.1, bf16[1024,1024]{1,0:T(8,128)(2,1)} %refs_1_.1, bf16[1024,1024]{1,0:T(8,128)(2,1)} %refs_2_.1, bf16[1024,1024]{1,0:T(8,128)(2,1)} %refs_3_.1, bf16[4096,1024]{1,0:T(8,128)(2,1)} %refs_4_.1, ...), custom_call_target="tpu_custom_call" | custom-call | flops 4000000000 | bytes 36000000 | tf_op jit(solution)/shard_map/pallas_call | solution.py:695
  56.7 2.3 %shard_map.201 = (bf16[32,1024]{1,0:T(8,128)(2,1)}, f32[64,1024]{1,0:T(8,128)}, f32[64,1024]{1,0:T(8,128)}, f32[64,1024]{1,0:T(8,128)}, f32[64,1024]{1,0:T(8,128)}) custom-call(bf16[32,1024]{1,0:T(8,128)(2,1)} %get-tuple-element.12.dec, f32[4,64,1024]{2,1,0:T(8,128)} %get-tuple-element.13.factors), custom_call_target="tpu_custom_call" | custom-call | tf_op jit(solution)/shard_map/pallas_call | solution.py:786
